TPU v7x, 32 devices: a whole 2x2x4 slice. The times are simulated.
32 devices in a mesh: pair: 8 (over y, x, core), col: 4 (over z).
Axes of the slice: x: 2, y: 2, z: 4, core: 2. Of those that a mesh axis runs over, the one named last changes fastest.
Arguments:
- tmatrix: bfloat16 [8, 2, 4096, 4096], P('pair', None, None, 'col'), may hold values from -0.046875 to 0.046875
- translation: bfloat16 [8, 2, 4096, 4096], P('pair', None, None, 'col'), may hold values from -0.0625 to 0.0625
- incident: bfloat16 [8, 4096, 256], P('pair', 'col'), may hold values from -6 to 6
- farfield: bfloat16 [2, 2048, 4096], P(None, None, 'col'), may hold values from -0.0625 to 0.0625
- centres: int32 [8, 3], replicated, may hold values from -8 to 8
Outputs:
- amplitude: float32 [8, 2048, 128], P('pair', 'col')
All inputs are finite; a program needn't handle non-finite values.
Results may differ from a plain program's by a relative error of at most 0.034.
Values may be sent and summed in bfloat16 or wider, within the bound.
A program may use at most 128 MiB of HBM per device.

v0:
```python
import math

import jax
import jax.numpy as jnp
from jax import lax
from jax.sharding import PartitionSpec as P

ITERS = 3
LEVEL = 2


def partner(value, axis, bit):
    mask = 2**bit
    pairs = [(source, source ^ mask) for source in range(lax.axis_size(axis))]
    return lax.ppermute(value, axis, pairs)


def turned_block(vector):
    half_width = vector.shape[1] // 2
    return jnp.concatenate([-vector[:, half_width:], vector[:, :half_width]], axis=1)


def rotate(field, phase):
    half_width = field.shape[1] // 2
    cosine = jnp.cos(phase)[:, None]
    sine = jnp.sin(phase)[:, None]
    real_part = field[:, :half_width]
    imag_part = field[:, half_width:]
    return jnp.concatenate(
        [cosine * real_part + sine * imag_part, cosine * imag_part - sine * real_part], axis=1
    )


def direction_phase(centre, count, total_rows):
    steps_int = jnp.arange(count, dtype=jnp.int32)
    polar = math.pi / total_rows * (steps_int.astype(jnp.float32) + 0.5)
    azimuth = 2.0 * math.pi / 97.0 * (steps_int * 40 % 97).astype(jnp.float32)
    spot = centre.astype(jnp.float32)
    return 0.7 * (
        jnp.sin(polar) * jnp.cos(azimuth) * spot[0]
        + jnp.sin(polar) * jnp.sin(azimuth) * spot[1]
        + jnp.cos(polar) * spot[2]
    )


def pick_half(vector, column_half, half_width):
    full_width = vector.shape[1] // 2
    real_part = lax.dynamic_slice_in_dim(vector, column_half * half_width, half_width, 1)
    imag_part = lax.dynamic_slice_in_dim(
        vector, full_width + column_half * half_width, half_width, 1
    )
    return jnp.concatenate([real_part, imag_part], axis=1)


def column_sums(operands):
    pieces = []
    for matrix, vector in operands:
        turned = turned_block(vector)
        real_rows = matrix[0]
        imag_rows = matrix[1]
        pieces.append(
            jnp.dot(real_rows, vector, preferred_element_type=jnp.float32)
            + jnp.dot(imag_rows, turned, preferred_element_type=jnp.float32)
        )
    return lax.psum_scatter(
        pieces[0].astype(jnp.bfloat16), "col", scatter_dimension=0, tiled=True
    ).astype(jnp.float32)


def far_sums(farfield, members):
    total_rows = farfield.shape[1]
    count = total_rows // lax.axis_size("col") * lax.axis_size("col")
    real_rows = farfield[0]
    imag_rows = farfield[1]
    summed = None
    for coeffs, centre in members:
        field = jnp.dot(real_rows, coeffs, preferred_element_type=jnp.float32) + jnp.dot(
            imag_rows, turned_block(coeffs), preferred_element_type=jnp.float32
        )
        turned_field = rotate(field, direction_phase(centre, count, total_rows))
        summed = turned_field
    return lax.psum_scatter(
        summed.astype(jnp.bfloat16), "col", scatter_dimension=0, tiled=True
    ).astype(jnp.float32)


def on_device(tmatrix, translation, incident, farfield, centres):
    pair_index = lax.axis_index("pair")
    column_half = jnp.bitwise_and(jnp.right_shift(pair_index, LEVEL), 1)
    own_centre = lax.dynamic_index_in_dim(centres, pair_index, 0, keepdims=False)
    own_matrix = tmatrix[0]
    own_coupling = translation[0]
    own_incident = incident[0]
    full_width = own_incident.shape[1] // 2
    half_width = full_width // 2
    coeffs = column_sums([(own_matrix, own_incident)]).astype(jnp.bfloat16)
    for iteration in range(ITERS):
        partner_coeffs = partner(coeffs, "pair", LEVEL)
        driven = (
            own_incident.astype(jnp.float32) + column_sums([(own_coupling, partner_coeffs)])
        ).astype(jnp.bfloat16)
        coeffs = column_sums([(own_matrix, driven)]).astype(jnp.bfloat16)
    own_field = far_sums(farfield, [(coeffs, own_centre)])
    outgoing = pick_half(own_field, 1 - column_half, half_width)
    incoming = partner(outgoing.astype(jnp.bfloat16), "pair", LEVEL).astype(outgoing.dtype)
    amplitude = pick_half(own_field, column_half, half_width) + incoming
    return amplitude[None]


def solution(mesh):
    return jax.shard_map(
        on_device,
        mesh=mesh,
        in_specs=(
            P("pair", None, None, "col"),
            P("pair", None, None, "col"),
            P("pair", "col", None),
            P(None, None, "col"),
            P(),
        ),
        out_specs=P("pair", "col", None),
        check_vma=False,
    )
```

profile of v0, /device:TPU:0, one launch (start us, length us, event | category | flops | bytes accessed | tf_op | source)
XLA Modules:
  0.0 507.0 jit_solution(9006484071926922288)
XLA Ops:
  7.8 8.1 %fusion.26 = f32[4096,256]{1,0:T(8,128)} fusion(bf16[1,2,4096,1024]{3,2,1,0:T(8,128)(2,1)} %param.5, bf16[1,1024,256]{2,1,0:T(8,128)(2,1)} %param.7), kind=kOutput, calls=%fused_computation.26 | convolution fusion | flops 2147483648 | bytes 13107200 | tf_op jit(solution)/shard_map/dot_general | solution.py:62
  15.9 1.7 copy-done.2
  17.7 6.2 %fusion.66 = bf16[4096,256]{1,0:T(8,128)(2,1)} fusion(f32[4096,256]{1,0:T(8,128)} %fusion.26, bf16[1,2,4096,1024]{3,2,1,0:T(8,128)(2,1)S(1)} %copy-done.2, bf16[1024,128]{0,1:T(8,128)(2,1)S(1)} %get-tuple-element.26, bf16[1024,128]{0,1:T(8,128)(2,1)S(1)} %get-tuple-element.25), kind=kOutput, calls=%fused_computation.50 | convolution fusion | flops 2150629376 | bytes 15204352 | tf_op jit(solution)/shard_map/dot_general | solution.py:63
  24.0 46.7 %reduce-scatter.9.cloned.1.call-done = bf16[1024,256]{1,0:T(8,128)(2,1)} async-done(((bf16[4096,256]{1,0:T(8,128)(2,1)}), bf16[1024,256]{1,0:T(8,128)(2,1)}) %reduce-scatter.9.cloned.1.call-update) | async-done | bytes 524304 | tf_op jit(solution)/shard_map/reduce_scatter | solution.py:65
  72.1 12.3 %collective-permute-done = bf16[1024,256]{1,0:T(8,128)(2,1)S(1)} collective-permute-done((bf16[1024,256]{1,0:T(8,128)(2,1)}, bf16[1024,256]{1,0:T(8,128)(2,1)S(1)}, u32[]{:S(2)}, u32[]{:S(2)}) %collective-permute-start) | collective-permute-done | bytes 524320 | tf_op jit(solution)/shard_map/ppermute | solution.py:15
  84.4 5.8 %fusion.4 = f32[256,4096]{1,0:T(8,128)S(1)} fusion(bf16[1,2,4096,1024]{3,2,1,0:T(8,128)(2,1)} %param.6, bf16[1024,128]{1,0:T(8,128)(2,1)S(1)} %get-tuple-element.24, bf16[1024,128]{1,0:T(8,128)(2,1)S(1)} %get-tuple-element.23), kind=kOutput, calls=%fused_computation.4 | convolution fusion | flops 2148532224 | bytes 13107200 | tf_op jit(solution)/shard_map/dot_general | solution.py:63
  90.2 7.3 %fusion.96 = bf16[4096,256]{0,1:T(8,128)(2,1)} fusion(f32[256,4096]{1,0:T(8,128)S(1)} %fusion.4, bf16[1024,256]{1,0:T(8,128)(2,1)S(1)} %collective-permute-done, bf16[1,2,4096,1024]{3,2,1,0:T(8,128)(2,1)} %param.6), kind=kOutput, calls=%fused_computation.60 | convolution fusion | flops 2149580800 | bytes 15204352 | tf_op jit(solution)/shard_map/dot_general | solution.py:62
  98.0 43.0 %reduce-scatter.11.cloned.1.call-done = bf16[1024,256]{0,1:T(8,128)(2,1)} async-done(((bf16[4096,256]{0,1:T(8,128)(2,1)}), bf16[1024,256]{0,1:T(8,128)(2,1)}) %reduce-scatter.11.cloned.1.call-update) | async-done | bytes 524304 | tf_op jit(solution)/shard_map/reduce_scatter | solution.py:65
  142.5 7.9 %fusion.16 = f32[256,4096]{1,0:T(8,128)} fusion(bf16[1,2,4096,1024]{3,2,1,0:T(8,128)(2,1)} %param.5, bf16[1024,128]{0,1:T(8,128)(2,1)S(1)} %get-tuple-element.22, bf16[1024,128]{0,1:T(8,128)(2,1)S(1)} %get-tuple-element.21), kind=kOutput, calls=%fused_computation.16 | convolution fusion | flops 2148532224 | bytes 13107200 | tf_op jit(solution)/shard_map/dot_general | solution.py:63
  150.4 6.0 %fusion.87 = bf16[4096,256]{0,1:T(8,128)(2,1)} fusion(f32[256,4096]{1,0:T(8,128)} %fusion.16, bf16[1024,256]{0,1:T(8,128)(2,1)S(1)} %fusion.117, bf16[1,2,4096,1024]{3,2,1,0:T(8,128)(2,1)S(1)} %bitcast.125), kind=kOutput, calls=%fused_computation.57 | convolution fusion | flops 2149580800 | bytes 15204352 | tf_op jit(solution)/shard_map/dot_general | solution.py:62
  156.5 43.3 %reduce-scatter.13.cloned.1.call-done = bf16[1024,256]{0,1:T(8,128)(2,1)} async-done(((bf16[4096,256]{0,1:T(8,128)(2,1)}), bf16[1024,256]{0,1:T(8,128)(2,1)}) %reduce-scatter.13.cloned.1.call-update) | async-done | bytes 524304 | tf_op jit(solution)/shard_map/reduce_scatter | solution.py:65
  199.8 1.5 collective-permute-start.1
  201.3 12.3 %collective-permute-done.1 = bf16[1024,256]{0,1:T(8,128)(2,1)S(1)} collective-permute-done((bf16[1024,256]{0,1:T(8,128)(2,1)}, bf16[1024,256]{0,1:T(8,128)(2,1)S(1)}, u32[]{:S(2)}, u32[]{:S(2)}) %collective-permute-start.1) | collective-permute-done | bytes 524320 | tf_op jit(solution)/shard_map/ppermute | solution.py:15
  213.6 5.8 %fusion.2 = f32[256,4096]{1,0:T(8,128)S(1)} fusion(bf16[1,2,4096,1024]{3,2,1,0:T(8,128)(2,1)} %param.6, bf16[1024,128]{0,1:T(8,128)(2,1)S(1)} %get-tuple-element.20, bf16[1024,128]{0,1:T(8,128)(2,1)S(1)} %get-tuple-element.19), kind=kOutput, calls=%fused_computation.2 | convolution fusion | flops 2148532224 | bytes 13107200 | tf_op jit(solution)/shard_map/dot_general | solution.py:63
  219.3 7.2 %fusion.99 = bf16[4096,256]{0,1:T(8,128)(2,1)} fusion(f32[256,4096]{1,0:T(8,128)S(1)} %fusion.2, bf16[1024,256]{0,1:T(8,128)(2,1)S(1)} %collective-permute-done.1, bf16[1,2,4096,1024]{3,2,1,0:T(8,128)(2,1)} %param.6), kind=kOutput, calls=%fused_computation.61 | convolution fusion | flops 2149580800 | bytes 15204352 | tf_op jit(solution)/shard_map/dot_general | solution.py:62
  226.8 43.3 %reduce-scatter.15.cloned.1.call-done = bf16[1024,256]{0,1:T(8,128)(2,1)} async-done(((bf16[4096,256]{0,1:T(8,128)(2,1)}), bf16[1024,256]{0,1:T(8,128)(2,1)}) %reduce-scatter.15.cloned.1.call-update) | async-done | bytes 524304 | tf_op jit(solution)/shard_map/reduce_scatter | solution.py:65
  271.6 7.9 %fusion.14 = f32[256,4096]{1,0:T(8,128)} fusion(bf16[1,2,4096,1024]{3,2,1,0:T(8,128)(2,1)} %param.5, bf16[1024,128]{0,1:T(8,128)(2,1)S(1)} %get-tuple-element.18, bf16[1024,128]{0,1:T(8,128)(2,1)S(1)} %get-tuple-element.17), kind=kOutput, calls=%fused_computation.14 | convolution fusion | flops 2148532224 | bytes 13107200 | tf_op jit(solution)/shard_map/dot_general | solution.py:63
  279.5 6.0 %fusion.90 = bf16[4096,256]{0,1:T(8,128)(2,1)} fusion(f32[256,4096]{1,0:T(8,128)} %fusion.14, bf16[1024,256]{0,1:T(8,128)(2,1)S(1)} %fusion.118, bf16[1,2,4096,1024]{3,2,1,0:T(8,128)(2,1)S(1)} %bitcast.127), kind=kOutput, calls=%fused_computation.58 | convolution fusion | flops 2149580800 | bytes 15204352 | tf_op jit(solution)/shard_map/dot_general | solution.py:62
  285.6 43.3 %reduce-scatter.17.cloned.1.call-done = bf16[1024,256]{0,1:T(8,128)(2,1)} async-done(((bf16[4096,256]{0,1:T(8,128)(2,1)}), bf16[1024,256]{0,1:T(8,128)(2,1)}) %reduce-scatter.17.cloned.1.call-update) | async-done | bytes 524304 | tf_op jit(solution)/shard_map/reduce_scatter | solution.py:65
  330.3 12.2 %collective-permute-done.2 = bf16[1024,256]{0,1:T(8,128)(2,1)S(1)} collective-permute-done((bf16[1024,256]{0,1:T(8,128)(2,1)}, bf16[1024,256]{0,1:T(8,128)(2,1)S(1)}, u32[]{:S(2)}, u32[]{:S(2)}) %collective-permute-start.2) | collective-permute-done | bytes 524320 | tf_op jit(solution)/shard_map/ppermute | solution.py:15
  342.6 5.8 %fusion = f32[256,4096]{1,0:T(8,128)S(1)} fusion(bf16[1,2,4096,1024]{3,2,1,0:T(8,128)(2,1)} %param.6, bf16[1024,128]{0,1:T(8,128)(2,1)S(1)} %get-tuple-element.16, bf16[1024,128]{0,1:T(8,128)(2,1)S(1)} %get-tuple-element.15), kind=kOutput, calls=%fused_computation | convolution fusion | flops 2148532224 | bytes 13107200 | tf_op jit(solution)/shard_map/dot_general | solution.py:63
  348.4 7.2 %fusion.102 = bf16[4096,256]{0,1:T(8,128)(2,1)} fusion(f32[256,4096]{1,0:T(8,128)S(1)} %fusion, bf16[1024,256]{0,1:T(8,128)(2,1)S(1)} %collective-permute-done.2, bf16[1,2,4096,1024]{3,2,1,0:T(8,128)(2,1)} %param.6), kind=kOutput, calls=%fused_computation.62 | convolution fusion | flops 2149580800 | bytes 15204352 | tf_op jit(solution)/shard_map/dot_general | solution.py:62
  355.8 43.3 %reduce-scatter.19.cloned.1.call-done = bf16[1024,256]{0,1:T(8,128)(2,1)} async-done(((bf16[4096,256]{0,1:T(8,128)(2,1)}), bf16[1024,256]{0,1:T(8,128)(2,1)}) %reduce-scatter.19.cloned.1.call-update) | async-done | bytes 524304 | tf_op jit(solution)/shard_map/reduce_scatter | solution.py:65
  400.4 5.7 %fusion.12 = f32[256,4096]{1,0:T(8,128)S(1)} fusion(bf16[1,2,4096,1024]{3,2,1,0:T(8,128)(2,1)} %param.5, bf16[1024,128]{0,1:T(8,128)(2,1)S(1)} %get-tuple-element.14, bf16[1024,128]{0,1:T(8,128)(2,1)S(1)} %get-tuple-element.13), kind=kOutput, calls=%fused_computation.12 | convolution fusion | flops 2148532224 | bytes 13107200 | tf_op jit(solution)/shard_map/dot_general | solution.py:63
  406.2 7.2 %fusion.93 = bf16[4096,256]{0,1:T(8,128)(2,1)} fusion(f32[256,4096]{1,0:T(8,128)S(1)} %fusion.12, bf16[1024,256]{0,1:T(8,128)(2,1)S(1)} %fusion.119, bf16[1,2,4096,1024]{3,2,1,0:T(8,128)(2,1)} %param.5), kind=kOutput, calls=%fused_computation.59 | convolution fusion | flops 2149580800 | bytes 15204352 | tf_op jit(solution)/shard_map/dot_general | solution.py:62
  414.1 2.1 fusion.166
  416.3 40.5 %reduce-scatter.21.cloned.1.call-done = bf16[1024,256]{0,1:T(8,128)(2,1)} async-done(((bf16[4096,256]{0,1:T(8,128)(2,1)}), bf16[1024,256]{0,1:T(8,128)(2,1)}) %reduce-scatter.21.cloned.1.call-update) | async-done | bytes 524304 | tf_op jit(solution)/shard_map/reduce_scatter | solution.py:65
  457.9 3.5 fusion.105
  461.4 3.5 fusion.114
  466.2 26.6 %reduce-scatter.23.cloned.1.call-done = bf16[512,256]{0,1:T(8,128)(2,1)} async-done(((bf16[2048,256]{0,1:T(8,128)(2,1)}), bf16[512,256]{0,1:T(8,128)(2,1)}) %reduce-scatter.23.cloned.1.call-update) | async-done | bytes 262160 | tf_op jit(solution)/shard_map/reduce_scatter | solution.py:82
  493.9 1.5 collective-permute-start.3
  495.5 3.6 collective-permute-done.3
  (63 shorter events, 14.8 us)
Async XLA Ops:
  6.5 64.1 %reduce-scatter.9.cloned.1.call-start = ((), (), s32[]{:S(2)}) async-start(), calls=%async_computation.8 | async-start | bytes 2621440 | tf_op jit(solution)/shard_map/reduce_scatter | solution.py:65
  7.8 9.8 %copy-start.2 = (bf16[1,2,4096,1024]{3,2,1,0:T(8,128)(2,1)S(1)}, bf16[1,2,4096,1024]{3,2,1,0:T(8,128)(2,1)}, u32[]{:S(2)}) copy-start(bf16[1,2,4096,1024]{3,2,1,0:T(8,128)(2,1)} %param.5) | copy-start | bytes 50331652
  23.9 117.1 %reduce-scatter.11.cloned.1.call-start = ((), (), s32[]{:S(2)}) async-start(), calls=%async_computation.9 | async-start | bytes 2621440 | tf_op jit(solution)/shard_map/reduce_scatter | solution.py:65
  70.6 13.7 %collective-permute-start = (bf16[1024,256]{1,0:T(8,128)(2,1)}, bf16[1024,256]{1,0:T(8,128)(2,1)S(1)}, u32[]{:S(2)}, u32[]{:S(2)}) collective-permute-start(bf16[1024,256]{1,0:T(8,128)(2,1)} %reduce-scatter.9.cloned.1.call-done), channel_id=1, source_target_pairs={{0,16},{4,20},{8,24},{12,28},{16,0},{20,4},{24,8},{28,12},{1,17},{... | collective-permute-start | bytes 1572872 | tf_op jit(solution)/shard_map/ppermute | solution.py:15
  97.5 102.3 %reduce-scatter.13.cloned.1.call-start = ((), (), s32[]{:S(2)}) async-start(), calls=%async_computation.10 | async-start | bytes 2621440 | tf_op jit(solution)/shard_map/reduce_scatter | solution.py:65
  141.0 9.3 %slice-start = ((s8[16777216]{0:T(1024)(128)(4,1)}), s8[4194304]{0:T(1024)(128)(4,1)S(1)}, s32[]{:S(2)}) async-start(s8[16777216]{0:T(1024)(128)(4,1)} %bitcast.124), calls=%async_computation.16 | async-start | bytes 8388608
  142.5 7.9 %slice-start.1 = ((s8[16777216]{0:T(1024)(128)(4,1)}), s8[4194304]{0:T(1024)(128)(4,1)S(1)}, s32[]{:S(2)}) async-start(s8[16777216]{0:T(1024)(128)(4,1)} %bitcast.124), calls=%async_computation.17 | async-start | bytes 8388608
  142.5 7.9 %slice-start.2 = ((s8[16777216]{0:T(1024)(128)(4,1)}), s8[4194304]{0:T(1024)(128)(4,1)S(1)}, s32[]{:S(2)}) async-start(s8[16777216]{0:T(1024)(128)(4,1)} %bitcast.124), calls=%async_computation.18 | async-start | bytes 8388608
  142.5 7.9 %slice-start.3 = ((s8[16777216]{0:T(1024)(128)(4,1)}), s8[4194304]{0:T(1024)(128)(4,1)S(1)}, s32[]{:S(2)}) async-start(s8[16777216]{0:T(1024)(128)(4,1)} %bitcast.124), calls=%async_computation.19 | async-start | bytes 8388608
  156.5 113.6 %reduce-scatter.15.cloned.1.call-start = ((), (), s32[]{:S(2)}) async-start(), calls=%async_computation.11 | async-start | bytes 2621440 | tf_op jit(solution)/shard_map/reduce_scatter | solution.py:65
  199.8 13.7 %collective-permute-start.1 = (bf16[1024,256]{0,1:T(8,128)(2,1)}, bf16[1024,256]{0,1:T(8,128)(2,1)S(1)}, u32[]{:S(2)}, u32[]{:S(2)}) collective-permute-start(bf16[1024,256]{0,1:T(8,128)(2,1)} %reduce-scatter.13.cloned.1.call-done), channel_id=1, source_target_pairs={{0,16},{4,20},{8,24},{12,28},{16,0},{20,4},{24,8},{28,12},{1,17},{... | collective-permute-start | bytes 1572872 | tf_op jit(solution)/shard_map/ppermute | solution.py:15
  226.5 102.3 %reduce-scatter.17.cloned.1.call-start = ((), (), s32[]{:S(2)}) async-start(), calls=%async_computation.12 | async-start | bytes 2621440 | tf_op jit(solution)/shard_map/reduce_scatter | solution.py:65
  270.1 9.3 %slice-start.4 = ((s8[16777216]{0:T(1024)(128)(4,1)}), s8[4194304]{0:T(1024)(128)(4,1)S(1)}, s32[]{:S(2)}) async-start(s8[16777216]{0:T(1024)(128)(4,1)} %bitcast.126), calls=%async_computation.20 | async-start | bytes 8388608
  271.5 7.9 %slice-start.5 = ((s8[16777216]{0:T(1024)(128)(4,1)}), s8[4194304]{0:T(1024)(128)(4,1)S(1)}, s32[]{:S(2)}) async-start(s8[16777216]{0:T(1024)(128)(4,1)} %bitcast.126), calls=%async_computation.21 | async-start | bytes 8388608
  271.5 7.9 %slice-start.6 = ((s8[16777216]{0:T(1024)(128)(4,1)}), s8[4194304]{0:T(1024)(128)(4,1)S(1)}, s32[]{:S(2)}) async-start(s8[16777216]{0:T(1024)(128)(4,1)} %bitcast.126), calls=%async_computation.22 | async-start | bytes 8388608
  271.6 7.9 %slice-start.7 = ((s8[16777216]{0:T(1024)(128)(4,1)}), s8[4194304]{0:T(1024)(128)(4,1)S(1)}, s32[]{:S(2)}) async-start(s8[16777216]{0:T(1024)(128)(4,1)} %bitcast.126), calls=%async_computation.23 | async-start | bytes 8388608
  285.5 113.6 %reduce-scatter.19.cloned.1.call-start = ((), (), s32[]{:S(2)}) async-start(), calls=%async_computation.13 | async-start | bytes 2621440 | tf_op jit(solution)/shard_map/reduce_scatter | solution.py:65
  328.9 13.7 %collective-permute-start.2 = (bf16[1024,256]{0,1:T(8,128)(2,1)}, bf16[1024,256]{0,1:T(8,128)(2,1)S(1)}, u32[]{:S(2)}, u32[]{:S(2)}) collective-permute-start(bf16[1024,256]{0,1:T(8,128)(2,1)} %reduce-scatter.17.cloned.1.call-done), channel_id=1, source_target_pairs={{0,16},{4,20},{8,24},{12,28},{16,0},{20,4},{24,8},{28,12},{1,17},{... | collective-permute-start | bytes 1572872 | tf_op jit(solution)/shard_map/ppermute | solution.py:15
  355.6 101.2 %reduce-scatter.21.cloned.1.call-start = ((), (), s32[]{:S(2)}) async-start(), calls=%async_computation.14 | async-start | bytes 2621440 | tf_op jit(solution)/shard_map/reduce_scatter | solution.py:65
  406.2 7.3 %copy-start.1 = (s32[8,3]{0,1:T(4,128)S(1)}, s32[8,3]{0,1:T(4,128)}, u32[]{:S(2)}) copy-start(s32[8,3]{0,1:T(4,128)} %param.9) | copy-start | bytes 292
  413.4 79.5 %reduce-scatter.23.cloned.1.call-start = ((), (), s32[]{:S(2)}) async-start(), calls=%async_computation.15 | async-start | bytes 1310720 | tf_op jit(solution)/shard_map/reduce_scatter | solution.py:82
  456.8 4.6 copy-start
  493.9 5.1 %collective-permute-start.3 = (bf16[512,128]{0,1:T(8,128)(2,1)S(1)}, bf16[512,128]{0,1:T(8,128)(2,1)S(1)}, u32[]{:S(2)}, u32[]{:S(2)}) collective-permute-start(bf16[512,128]{0,1:T(8,128)(2,1)S(1)} %pad_maximum_fusion.1), channel_id=1, source_target_pairs={{0,16},{4,20},{8,24},{12,28},{16,0},{20,4},{24,8},{28,12},{1,17},{... | collective-permute-start | bytes 393224 | tf_op jit(solution)/shard_map/ppermute | solution.py:15
Sparse Core Ops, SparseCore 0:
  24.0 46.5 reduce-scatter.8
  97.6 43.3 reduce-scatter.10
  156.6 43.1 reduce-scatter.12
  226.7 43.3 reduce-scatter.14
  285.6 43.1 reduce-scatter.16
  355.7 43.3 reduce-scatter.18
  413.5 43.1 reduce-scatter.20
  466.4 26.4 reduce-scatter.22
where the time goes:
time: 515 us; the launch traced here: 507 us
  waiting for transfers between devices  371 us (72%)
  matrix products  101 us (20%)
  between operations  14 us (3%)
  other arithmetic  9.98 us (2%)
  starting transfers between devices  7.06 us (1%)
    reduce_scatter x7, waiting for transfers between devices, column_sums(): lax.psum_scatter(pieces[0].astype(jnp.bfloat16), 'col', scatter_dimension...  303 us
    dot_general x7, matrix products, column_sums(): jnp.dot(real_rows, vector, preferred_element_type=jnp.float32)  48.9 us
    dot_general x7, matrix products, column_sums(): jnp.dot(imag_rows, turned, preferred_element_type=jnp.float32)  45 us
    ppermute x4, waiting for transfers between devices, partner(): return lax.ppermute(value, axis, pairs)  40.3 us
    reduce_scatter x1, waiting for transfers between devices, far_sums(): lax.psum_scatter(summed.astype(jnp.bfloat16), 'col', scatter_dimension=0,...  26.6 us
  transfers between devices with their start and end apart: 12, of which 12 were waited for; matrix products, arithmetic and copies ran while one was open for 1% of the time, Pallas kernels for 0%

commit v1 on v0

v1 whole, which is shorter than its diff:
```python
import functools
import math

import jax
import jax.numpy as jnp
from jax import lax
from jax.experimental import pallas as pl
from jax.experimental.pallas import tpu as pltpu
from jax.sharding import PartitionSpec as P

ITERS = 3
LEVEL = 2
MESH = pl.DeviceIdType.MESH
BF16 = jnp.bfloat16
F32 = jnp.float32
CHUNKS = 4
LAG = 2


def direction_phase(centre, total_rows):
    steps_int = jnp.arange(total_rows, dtype=jnp.int32)
    polar = math.pi / total_rows * (steps_int.astype(F32) + 0.5)
    azimuth = 2.0 * math.pi / 97.0 * (steps_int * 40 % 97).astype(F32)
    spot = centre.astype(F32)
    return 0.7 * (
        jnp.sin(polar) * jnp.cos(azimuth) * spot[0]
        + jnp.sin(polar) * jnp.sin(azimuth) * spot[1]
        + jnp.cos(polar) * spot[2]
    )


def dot(a, b):
    return jnp.dot(a, b, preferred_element_type=F32)


def kernel(
    n, tm, tr, ff, e_ref, cos_ref, sin_ref, out_ref,
    w, f, xs, xsrc, abuf, part, recv, fpart, frecv,
    wsem, fsem, ssem, rsem, psem, qsem, fssem, frsem,
):
    Q = CHUNKS
    c = lax.axis_index("col")
    g = lax.axis_index("pair")
    half = (g // 2**LEVEL) % 2
    other = g + 2**LEVEL * (1 - 2 * half)
    rows, width = e_ref.shape
    full = width // 2
    cr = rows // Q
    fr = out_ref.shape[0] // Q
    sends = (n - 1) * Q

    n_right, n_left = n - 1 - c, c
    prim_right = n_right > n_left
    n_sec = jnp.minimum(n_right, n_left) * Q

    def step(i):
        k = jnp.maximum(i - LAG, 0)
        mid = (i >= LAG) & (k < 2 * n_sec)
        sec = mid & (k % 2 == 0)
        pri_idx = jnp.where(i < LAG, i, jnp.where(mid, LAG + k // 2, i - n_sec))
        idx = jnp.where(sec, k // 2, pri_idx)
        right = jnp.where(sec, jnp.where(prim_right, 0, 1), jnp.where(prim_right, 1, 0))
        j, q = idx // Q, idx % Q
        d = jnp.where(right == 1, n - 1 - j, j)
        target = jnp.where(right == 1, c + 1, c - 1)
        has_in = jnp.where(right == 1, c > 0, c < n - 1)
        slot_out = jnp.where((right == 0) & (d == target), n, d)
        return d, q, target, has_in, slot_out

    def order(i):
        own = i >= sends
        d, q, _, _, _ = step(jnp.minimum(i, sends - 1))
        return jnp.where(own, c, d), jnp.where(own, i - sends, q)

    def w_copy(which, i):
        d, q = order(i)
        src = tm if which == 0 else tr
        at = pl.ds(pl.multiple_of(d * rows + q * cr, cr), cr)
        return pltpu.make_async_copy(src.at[0, :, at, :], w.at[which, :, at, :], wsem.at[which, i])

    for which in range(2):

        def load(i, _, which=which):
            w_copy(which, i).start()
            return 0

        lax.fori_loop(0, n * Q, load, 0)
    f_copy = pltpu.make_async_copy(ff, f, fsem)
    f_copy.start()

    barrier = pltpu.get_barrier_semaphore()

    @pl.when(c > 0)
    def _():
        pl.semaphore_signal(barrier, inc=1, device_id={"col": c - 1}, device_id_type=MESH)

    @pl.when(c < n - 1)
    def _():
        pl.semaphore_signal(barrier, inc=1, device_id={"col": c + 1}, device_id_type=MESH)

    pl.semaphore_signal(barrier, inc=1, device_id={"pair": other}, device_id_type=MESH)
    pl.semaphore_wait(
        barrier, 1 + jnp.where(c > 0, 1, 0) + jnp.where(c < n - 1, 1, 0)
    )

    def send_copy(par, i, d, q, target, slot_out):
        return pltpu.make_async_remote_copy(
            src_ref=part.at[par, d, q],
            dst_ref=recv.at[par, slot_out, q],
            send_sem=ssem.at[par, i],
            recv_sem=rsem.at[par, slot_out, q],
            device_id={"col": target},
            device_id_type=MESH,
        )

    def arrived(par, slot, q):
        pltpu.make_async_copy(
            recv.at[par, slot, q], recv.at[par, slot, q], rsem.at[par, slot, q]
        ).wait()

    def pair_copy(ex, q):
        at = pl.ds(pl.multiple_of(q * cr, cr), cr)
        return pltpu.make_async_remote_copy(
            src_ref=abuf.at[at, :],
            dst_ref=xsrc.at[ex % 2, at, :],
            send_sem=psem.at[ex % 2, q],
            recv_sem=qsem.at[ex % 2, q],
            device_id={"pair": other},
            device_id_type=MESH,
        )

    def turn(x):
        xs[0:rows, :] = x
        xs[rows : 2 * rows, 0:full] = -x[:, full:]
        xs[rows : 2 * rows, full:] = x[:, :full]

    def product(which, d, q):
        at = pl.ds(pl.multiple_of(d * rows + q * cr, cr), cr)
        return dot(w[which, 0, at, :], xs[0:rows, :]) + dot(w[which, 1, at, :], xs[rows:, :])

    xsrc[2] = e_ref[...]

    def one_product(p, _):
        which = p % 2
        par = p % 2
        ex = p // 2

        @pl.when(which == 1)
        def _():
            def wait_pair(q, _):
                pair_copy(ex, q).wait()
                return 0

            lax.fori_loop(0, Q, wait_pair, 0)
            turn(xsrc[ex % 2])

        @pl.when(which == 0)
        def _():
            turn(xsrc[2])

        def loaded(i):
            @pl.when(p == 0)
            def _():
                w_copy(0, i).wait()

            @pl.when(p == 1)
            def _():
                w_copy(1, i).wait()

        def send_step(i, _):
            d, q, target, has_in, slot_out = step(i)
            loaded(i)
            value = product(which, d, q)
            copy = send_copy(par, i, d, q, target, slot_out)

            @pl.when(p >= 2)
            def _():
                copy.wait_send()

            @pl.when(has_in)
            def _():
                arrived(par, d, q)
                part[par, d, q] = (value + recv[par, d, q].astype(F32)).astype(BF16)

            @pl.when(jnp.logical_not(has_in))
            def _():
                part[par, d, q] = value.astype(BF16)

            copy.start()
            return 0

        lax.fori_loop(0, sends, send_step, 0)

        def own_step(q, _):
            loaded(sends + q)
            at = pl.ds(pl.multiple_of(q * cr, cr), cr)
            value = product(which, c, q)

            @pl.when(c == 0)
            def _():
                arrived(par, n, q)
                finish(value + recv[par, n, q].astype(F32), q, at)

            @pl.when(c == n - 1)
            def _():
                arrived(par, c, q)
                finish(value + recv[par, c, q].astype(F32), q, at)

            @pl.when((c > 0) & (c < n - 1))
            def _():
                arrived(par, n, q)
                arrived(par, c, q)
                finish(
                    value + recv[par, c, q].astype(F32) + recv[par, n, q].astype(F32), q, at
                )

            return 0

        def finish(value, q, at):
            @pl.when(which == 1)
            def _():
                xsrc[2, at, :] = (value + e_ref[at, :].astype(F32)).astype(BF16)

            @pl.when(which == 0)
            def _():
                abuf[at, :] = value.astype(BF16)
                pair_copy(ex, q).start()

        lax.fori_loop(0, Q, own_step, 0)
        return 0

    products = 2 * ITERS + 1
    lax.fori_loop(0, products, one_product, 0)

    last = ITERS

    def wait_pair(q, _):
        pair_copy(last, q).wait()
        return 0

    lax.fori_loop(0, Q, wait_pair, 0)
    kh = full // 2

    def halves(lo):
        a = abuf[...].astype(F32)
        b = xsrc[last % 2].astype(F32)
        re = jnp.concatenate([a[:, lo : lo + kh], b[:, lo : lo + kh]], axis=1)
        im = jnp.concatenate(
            [a[:, full + lo : full + lo + kh], b[:, full + lo : full + lo + kh]], axis=1
        )
        turn(jnp.concatenate([re, im], axis=1).astype(BF16))

    @pl.when(half == 0)
    def _():
        halves(0)

    @pl.when(half == 1)
    def _():
        halves(kh)

    f_copy.wait()

    def far(d, q):
        at = pl.ds(pl.multiple_of((d * Q + q) * fr, fr), fr)
        field = dot(f[0, at, :], xs[0:rows, :]) + dot(f[1, at, :], xs[rows:, :])
        cosine, sine = cos_ref[at, :], sin_ref[at, :]
        real, imag = field[:, :full], field[:, full:]
        re = cosine * real + sine * imag
        im = cosine * imag - sine * real
        return jnp.concatenate([re[:, :kh] + re[:, kh:], im[:, :kh] + im[:, kh:]], axis=1)

    def far_copy(i, d, q, target, slot_out):
        return pltpu.make_async_remote_copy(
            src_ref=fpart.at[d, q],
            dst_ref=frecv.at[slot_out, q],
            send_sem=fssem.at[i],
            recv_sem=frsem.at[slot_out, q],
            device_id={"col": target},
            device_id_type=MESH,
        )

    def far_arrived(slot, q):
        pltpu.make_async_copy(frecv.at[slot, q], frecv.at[slot, q], frsem.at[slot, q]).wait()

    def far_step(i, _):
        d, q, target, has_in, slot_out = step(i)
        value = far(d, q)

        @pl.when(has_in)
        def _():
            far_arrived(d, q)
            fpart[d, q] = (value + frecv[d, q].astype(F32)).astype(BF16)

        @pl.when(jnp.logical_not(has_in))
        def _():
            fpart[d, q] = value.astype(BF16)

        far_copy(i, d, q, target, slot_out).start()
        return 0

    lax.fori_loop(0, sends, far_step, 0)

    def far_own(q, _):
        at = pl.ds(pl.multiple_of(q * fr, fr), fr)
        out_ref[at, :] = far(c, q)

        @pl.when(c > 0)
        def _():
            far_arrived(c, q)
            out_ref[at, :] += frecv[c, q].astype(F32)

        @pl.when(c < n - 1)
        def _():
            far_arrived(n, q)
            out_ref[at, :] += frecv[n, q].astype(F32)

        return 0

    lax.fori_loop(0, Q, far_own, 0)

    def drain(i, _):
        d, q, target, _, slot_out = step(i)
        send_copy(0, i, d, q, target, slot_out).wait_send()
        send_copy(1, i, d, q, target, slot_out).wait_send()
        far_copy(i, d, q, target, slot_out).wait_send()
        return 0

    lax.fori_loop(0, sends, drain, 0)


def on_device(n, tmatrix, translation, incident, farfield, centres):
    pair_index = lax.axis_index("pair")
    other = jnp.bitwise_xor(pair_index, 2**LEVEL)
    own_incident = incident[0]
    rows, width = own_incident.shape
    total_rows = farfield.shape[1]
    block = total_rows // n
    full = width // 2
    kh = full // 2
    Q = CHUNKS
    spots = jnp.stack(
        [
            lax.dynamic_index_in_dim(centres, pair_index, 0, keepdims=False),
            lax.dynamic_index_in_dim(centres, other, 0, keepdims=False),
        ]
    )
    phases = [direction_phase(spots[m], total_rows) for m in range(2)]

    def lanes(fn):
        return jnp.concatenate(
            [jnp.broadcast_to(fn(phase)[:, None], (total_rows, kh)) for phase in phases], axis=1
        )

    vmem = pl.BlockSpec(memory_space=pltpu.VMEM)
    hbm = pl.BlockSpec(memory_space=pl.ANY)
    dma = pltpu.SemaphoreType.DMA
    out = pl.pallas_call(
        functools.partial(kernel, n),
        out_shape=jax.ShapeDtypeStruct((block, full), F32),
        in_specs=[hbm, hbm, hbm, vmem, vmem, vmem],
        out_specs=vmem,
        scratch_shapes=[
            pltpu.VMEM((2, 2, n * rows, rows), BF16),
            pltpu.VMEM(farfield.shape, BF16),
            pltpu.VMEM((2 * rows, width), BF16),
            pltpu.VMEM((3, rows, width), BF16),
            pltpu.VMEM((rows, width), BF16),
            pltpu.VMEM((2, n, Q, rows // Q, width), BF16),
            pltpu.VMEM((2, n + 1, Q, rows // Q, width), BF16),
            pltpu.VMEM((n, Q, block // Q, full), BF16),
            pltpu.VMEM((n + 1, Q, block // Q, full), BF16),
            dma((2, n * Q)),
            dma,
            dma((2, (n - 1) * Q)),
            dma((2, n + 1, Q)),
            dma((2, Q)),
            dma((2, Q)),
            dma(((n - 1) * Q,)),
            dma((n + 1, Q)),
        ],
        compiler_params=pltpu.CompilerParams(
            collective_id=0, has_side_effects=True, vmem_limit_bytes=63 * 2**20
        ),
    )(tmatrix, translation, farfield, own_incident, lanes(jnp.cos), lanes(jnp.sin))
    return out[None]


def solution(mesh):
    return jax.shard_map(
        functools.partial(on_device, mesh.shape["col"]),
        mesh=mesh,
        in_specs=(
            P("pair", None, None, "col"),
            P("pair", None, None, "col"),
            P("pair", "col", None),
            P(None, None, "col"),
            P(),
        ),
        out_specs=P("pair", "col", None),
        check_vma=False,
    )
```

time: 515 us -> 278 us (0.54); the launches traced: 507 us -> 277 us
  waiting for transfers between devices: 371 us -> 0 us
  Pallas kernels: 0 us -> 262 us
  matrix products: 101 us -> 0 us
  between operations: 14 us -> 0.04 us
  starting transfers between devices: 7.06 us -> 0 us
    reduce_scatter x8 -> x0, waiting for transfers between devices: 330 us -> none  [the longest x7 303 us: column_sums(): lax.psum_scatter(pieces[0].astype(jnp.bfloat16), 'col', scatter_dimension...]
    pallas_call x0 -> x1, Pallas kernels: none -> 262 us  [on_device(): pl.pallas_call(functools.partial(kernel, n), out_shape=jax.ShapeDtypeStru...]
    dot_general x16 -> x0, matrix products: 101 us -> none  [the longest x7 48.9 us: column_sums(): jnp.dot(real_rows, vector, preferred_element_type=jnp.float32)]
    ppermute x4 -> x0, waiting for transfers between devices: 40.3 us -> none  [partner(): return lax.ppermute(value, axis, pairs)]
    ppermute x4 -> x0, starting transfers between devices: 5.92 us -> none  [partner(): return lax.ppermute(value, axis, pairs)]
  transfers between devices with their start and end apart: 12 -> 0, of which waited for: 12 -> 0; matrix products, arithmetic and copies ran while one was open for 1% -> 0% of each run, Pallas kernels for 0% -> 0%
where the time goes in v1:
time: 278 us; the launch traced here: 277 us
  Pallas kernels  262 us (94%)
  other arithmetic  11.6 us (4%)
  local copies, waits for them, and re-layouts  3.58 us (1%)
    pallas_call x1, Pallas kernels, on_device(): pl.pallas_call(functools.partial(kernel, n), out_shape=jax.ShapeDtypeStru...  262 us

profile of v1, /device:TPU:0, one launch (start us, length us, event | category | flops | bytes accessed | tf_op | source)
XLA Modules:
  0.0 277.1 jit_solution(15161138223635703554)
XLA Ops:
  0.0 0.8 dynamic-slice_convert_fusion.1
  0.8 0.6 fusion.24
  1.4 2.0 fusion.22
  3.5 0.3 broadcast_in_dim.12
  3.8 2.0 fusion.20
  5.8 0.3 broadcast_in_dim.13
  6.1 1.3 pad_maximum_fusion.1.sin_ref
  7.5 2.0 fusion.23
  9.5 0.3 broadcast_in_dim.10
  9.8 2.0 fusion.21
  11.8 0.3 broadcast_in_dim.11
  12.2 1.4 pad_maximum_fusion.cos_ref
  13.5 261.9 %shard_map.55 = f32[512,128]{1,0:T(8,128)} custom-call(bf16[1,2,4096,1024]{3,2,1,0:T(8,128)(2,1)} %tm.1, bf16[1,2,4096,1024]{3,2,1,0:T(8,128)(2,1)} %tr.1, bf16[2,2048,1024]{2,1,0:T(8,128)(2,1)} %ff.1, bf16[1024,256]{1,0:T(8,128)(2,1)} %bitcast.9, f32[2048,128]{1,0:T(8,128)} %pad_maximum_fusion.cos_ref, f32[2048,128]{1,0:T(8,128)} %pad_maximum_fusion.1.sin_ref), custom_call_target="tpu_custom_call" | custom-call | tf_op jit(solution)/shard_map/pallas_call | solution.py:357
  275.4 1.7 copy.7

commit v2 on v1

--- a/solution.py
+++ b/solution.py
@@ -17,26 +17,14 @@
 LAG = 2
 
 
-def direction_phase(centre, total_rows):
-    steps_int = jnp.arange(total_rows, dtype=jnp.int32)
-    polar = math.pi / total_rows * (steps_int.astype(F32) + 0.5)
-    azimuth = 2.0 * math.pi / 97.0 * (steps_int * 40 % 97).astype(F32)
-    spot = centre.astype(F32)
-    return 0.7 * (
-        jnp.sin(polar) * jnp.cos(azimuth) * spot[0]
-        + jnp.sin(polar) * jnp.sin(azimuth) * spot[1]
-        + jnp.cos(polar) * spot[2]
-    )
-
-
 def dot(a, b):
     return jnp.dot(a, b, preferred_element_type=F32)
 
 
 def kernel(
-    n, tm, tr, ff, e_ref, cos_ref, sin_ref, out_ref,
-    w, f, xs, xsrc, abuf, part, recv, fpart, frecv,
-    wsem, fsem, ssem, rsem, psem, qsem, fssem, frsem,
+    n, tm, tr, ff, e_hbm, centres, out_ref,
+    w, f, e_ref, xs, xsrc, abuf, part, recv, fpart, frecv, trig, cos_ref, sin_ref,
+    wsem, fsem, esem, ssem, rsem, psem, qsem, fssem, frsem,
 ):
     Q = CHUNKS
     c = lax.axis_index("col")
@@ -78,6 +66,8 @@
         at = pl.ds(pl.multiple_of(d * rows + q * cr, cr), cr)
         return pltpu.make_async_copy(src.at[0, :, at, :], w.at[which, :, at, :], wsem.at[which, i])
 
+    e_copy = pltpu.make_async_copy(e_hbm.at[0], e_ref, esem)
+    e_copy.start()
     for which in range(2):
 
         def load(i, _, which=which):
@@ -117,6 +107,17 @@
         pltpu.make_async_copy(
             recv.at[par, slot, q], recv.at[par, slot, q], rsem.at[par, slot, q]
         ).wait()
+
+    def half_copy(q):
+        at = pl.ds(pl.multiple_of(q * cr, cr), cr)
+        return pltpu.make_async_remote_copy(
+            src_ref=abuf.at[at, 0:full],
+            dst_ref=xsrc.at[ITERS % 2, at, 0:full],
+            send_sem=psem.at[ITERS % 2, q],
+            recv_sem=qsem.at[ITERS % 2, q],
+            device_id={"pair": other},
+            device_id_type=MESH,
+        )
 
     def pair_copy(ex, q):
         at = pl.ds(pl.multiple_of(q * cr, cr), cr)
@@ -138,7 +139,40 @@
         at = pl.ds(pl.multiple_of(d * rows + q * cr, cr), cr)
         return dot(w[which, 0, at, :], xs[0:rows, :]) + dot(w[which, 1, at, :], xs[rows:, :])
 
-    xsrc[2] = e_ref[...]
+    total_rows = f.shape[1]
+    lanes = trig.shape[2]
+
+    def phase_values():
+        shape = (total_rows // lanes, lanes)
+        s = lax.broadcasted_iota(jnp.int32, shape, 0) * lanes
+        s = (s + lax.broadcasted_iota(jnp.int32, shape, 1)).astype(F32)
+        polar = math.pi / total_rows * (s + 0.5)
+        turns = 40.0 * s
+        rest = turns - 97.0 * jnp.floor((turns + 0.5) * (1.0 / 97.0))
+        azimuth = 2.0 * math.pi / 97.0 * rest
+        ux = jnp.sin(polar) * jnp.cos(azimuth)
+        uy = jnp.sin(polar) * jnp.sin(azimuth)
+        uz = jnp.cos(polar)
+        for m, member in enumerate((g, other)):
+            spot = [centres[member, axis].astype(F32) for axis in range(3)]
+            phase = 0.7 * (ux * spot[0] + uy * spot[1] + uz * spot[2])
+            trig[m] = jnp.cos(phase)
+            trig[2 + m] = jnp.sin(phase)
+
+    def spread(r, _):
+        at = pl.ds(pl.multiple_of(r * lanes, lanes), lanes)
+        for first, table in ((0, cos_ref), (2, sin_ref)):
+            both = [
+                jnp.broadcast_to(trig[first + m, pl.ds(r, 1), :], (full // 2, lanes))
+                for m in range(2)
+            ]
+            table[at, :] = jnp.concatenate(both, axis=0).T
+        return 0
+
+    e_copy.wait()
+
+    last_product = 2 * ITERS
+    kh = full // 2
 
     def one_product(p, _):
         which = p % 2
@@ -156,7 +190,13 @@
 
         @pl.when(which == 0)
         def _():
-            turn(xsrc[2])
+            @pl.when(p == 0)
+            def _():
+                turn(e_ref[...])
+
+            @pl.when(p > 0)
+            def _():
+                turn(xsrc[2])
 
         def loaded(i):
             @pl.when(p == 0)
@@ -191,6 +231,14 @@
 
         lax.fori_loop(0, sends, send_step, 0)
 
+        @pl.when(p == 2)
+        def _():
+            phase_values()
+
+        @pl.when(p == 3)
+        def _():
+            lax.fori_loop(0, total_rows // lanes, spread, 0)
+
         def own_step(q, _):
             loaded(sends + q)
             at = pl.ds(pl.multiple_of(q * cr, cr), cr)
@@ -221,43 +269,36 @@
             def _():
                 xsrc[2, at, :] = (value + e_ref[at, :].astype(F32)).astype(BF16)
 
-            @pl.when(which == 0)
+            @pl.when((which == 0) & (p < last_product))
             def _():
                 abuf[at, :] = value.astype(BF16)
                 pair_copy(ex, q).start()
 
+            @pl.when(p == last_product)
+            def _():
+                low = jnp.concatenate([value[:, :kh], value[:, full : full + kh]], axis=1)
+                high = jnp.concatenate([value[:, kh:full], value[:, full + kh :]], axis=1)
+                abuf[at, 0:full] = jnp.where(half == 0, high, low).astype(BF16)
+                abuf[at, full:] = jnp.where(half == 0, low, high).astype(BF16)
+                half_copy(q).start()
+
         lax.fori_loop(0, Q, own_step, 0)
         return 0
 
-    products = 2 * ITERS + 1
-    lax.fori_loop(0, products, one_product, 0)
-
-    last = ITERS
-
-    def wait_pair(q, _):
-        pair_copy(last, q).wait()
-        return 0
-
-    lax.fori_loop(0, Q, wait_pair, 0)
-    kh = full // 2
-
-    def halves(lo):
-        a = abuf[...].astype(F32)
-        b = xsrc[last % 2].astype(F32)
-        re = jnp.concatenate([a[:, lo : lo + kh], b[:, lo : lo + kh]], axis=1)
-        im = jnp.concatenate(
-            [a[:, full + lo : full + lo + kh], b[:, full + lo : full + lo + kh]], axis=1
-        )
-        turn(jnp.concatenate([re, im], axis=1).astype(BF16))
-
-    @pl.when(half == 0)
-    def _():
-        halves(0)
-
-    @pl.when(half == 1)
-    def _():
-        halves(kh)
-
+    lax.fori_loop(0, last_product + 1, one_product, 0)
+
+    def wait_half(q, _):
+        half_copy(q).wait()
+        return 0
+
+    lax.fori_loop(0, Q, wait_half, 0)
+    own = abuf[:, full:].astype(F32)
+    theirs = xsrc[ITERS % 2, :, 0:full].astype(F32)
+    turn(
+        jnp.concatenate(
+            [own[:, :kh], theirs[:, :kh], own[:, kh:], theirs[:, kh:]], axis=1
+        ).astype(BF16)
+    )
     f_copy.wait()
 
     def far(d, q):
@@ -329,39 +370,23 @@
 
 
 def on_device(n, tmatrix, translation, incident, farfield, centres):
-    pair_index = lax.axis_index("pair")
-    other = jnp.bitwise_xor(pair_index, 2**LEVEL)
-    own_incident = incident[0]
-    rows, width = own_incident.shape
+    _, rows, width = incident.shape
     total_rows = farfield.shape[1]
     block = total_rows // n
     full = width // 2
-    kh = full // 2
     Q = CHUNKS
-    spots = jnp.stack(
-        [
-            lax.dynamic_index_in_dim(centres, pair_index, 0, keepdims=False),
-            lax.dynamic_index_in_dim(centres, other, 0, keepdims=False),
-        ]
-    )
-    phases = [direction_phase(spots[m], total_rows) for m in range(2)]
-
-    def lanes(fn):
-        return jnp.concatenate(
-            [jnp.broadcast_to(fn(phase)[:, None], (total_rows, kh)) for phase in phases], axis=1
-        )
-
     vmem = pl.BlockSpec(memory_space=pltpu.VMEM)
     hbm = pl.BlockSpec(memory_space=pl.ANY)
     dma = pltpu.SemaphoreType.DMA
     out = pl.pallas_call(
         functools.partial(kernel, n),
         out_shape=jax.ShapeDtypeStruct((block, full), F32),
-        in_specs=[hbm, hbm, hbm, vmem, vmem, vmem],
+        in_specs=[hbm, hbm, hbm, hbm, pl.BlockSpec(memory_space=pltpu.SMEM)],
         out_specs=vmem,
         scratch_shapes=[
             pltpu.VMEM((2, 2, n * rows, rows), BF16),
             pltpu.VMEM(farfield.shape, BF16),
+            pltpu.VMEM((rows, width), BF16),
             pltpu.VMEM((2 * rows, width), BF16),
             pltpu.VMEM((3, rows, width), BF16),
             pltpu.VMEM((rows, width), BF16),
@@ -369,7 +394,11 @@
             pltpu.VMEM((2, n + 1, Q, rows // Q, width), BF16),
             pltpu.VMEM((n, Q, block // Q, full), BF16),
             pltpu.VMEM((n + 1, Q, block // Q, full), BF16),
+            pltpu.VMEM((4, total_rows // 128, 128), F32),
+            pltpu.VMEM((total_rows, full), F32),
+            pltpu.VMEM((total_rows, full), F32),
             dma((2, n * Q)),
+            dma,
             dma,
             dma((2, (n - 1) * Q)),
             dma((2, n + 1, Q)),
@@ -381,7 +410,7 @@
         compiler_params=pltpu.CompilerParams(
             collective_id=0, has_side_effects=True, vmem_limit_bytes=63 * 2**20
         ),
-    )(tmatrix, translation, farfield, own_incident, lanes(jnp.cos), lanes(jnp.sin))
+    )(tmatrix, translation, farfield, incident, centres)
     return out[None]
 
 

time: 278 us -> 264 us (0.950)
  other arithmetic: 11.6 us -> 0 us
    sin x2 -> x0, other arithmetic: 4.04 us -> none  [lanes(): fn(phase)[:, None]]
    cos x2 -> x0, other arithmetic: 4.04 us -> none  [lanes(): fn(phase)[:, None]]
where the time goes in v2:
time: 264 us
  Pallas kernels  261 us (99%)
  local copies, waits for them, and re-layouts  3.02 us (1%)
    pallas_call x1, Pallas kernels, on_device(): pl.pallas_call(functools.partial(kernel, n), out_shape=jax.ShapeDtypeStru...  261 us

profile of v2, /device:TPU:0, one launch (start us, length us, event | category | flops | bytes accessed | tf_op | source)
XLA Modules:
  0.0 263.6 jit_solution(15977103492218602382)
XLA Ops:
  0.0 1.3 copy.6.centres
  1.3 260.6 %shard_map.55 = f32[512,128]{1,0:T(8,128)} custom-call(bf16[1,2,4096,1024]{3,2,1,0:T(8,128)(2,1)} %tm.1, bf16[1,2,4096,1024]{3,2,1,0:T(8,128)(2,1)} %tr.1, bf16[2,2048,1024]{2,1,0:T(8,128)(2,1)} %ff.1, bf16[1,1024,256]{2,1,0:T(8,128)(2,1)} %e_hbm.1, s32[8,3]{1,0:T(8,128)} %copy.6.centres), custom_call_target="tpu_custom_call" | custom-call | tf_op jit(solution)/shard_map/pallas_call | solution.py:381
  261.9 1.7 copy.8

commit v3 on v2

--- a/solution.py
+++ b/solution.py
@@ -14,7 +14,7 @@
 BF16 = jnp.bfloat16
 F32 = jnp.float32
 CHUNKS = 4
-LAG = 2
+LAG = 4
 
 
 def dot(a, b):
@@ -134,6 +134,13 @@
         xs[0:rows, :] = x
         xs[rows : 2 * rows, 0:full] = -x[:, full:]
         xs[rows : 2 * rows, full:] = x[:, :full]
+
+    def turn_chunk(x, q):
+        at = pl.ds(pl.multiple_of(q * cr, cr), cr)
+        below = pl.ds(pl.multiple_of(rows + q * cr, cr), cr)
+        xs[at, :] = x
+        xs[below, 0:full] = -x[:, full:]
+        xs[below, full:] = x[:, :full]
 
     def product(which, d, q):
         at = pl.ds(pl.multiple_of(d * rows + q * cr, cr), cr)
@@ -183,10 +190,10 @@
         def _():
             def wait_pair(q, _):
                 pair_copy(ex, q).wait()
+                turn_chunk(xsrc[ex % 2, pl.ds(pl.multiple_of(q * cr, cr), cr), :], q)
                 return 0
 
             lax.fori_loop(0, Q, wait_pair, 0)
-            turn(xsrc[ex % 2])
 
         @pl.when(which == 0)
         def _():
@@ -289,16 +296,14 @@
 
     def wait_half(q, _):
         half_copy(q).wait()
+        at = pl.ds(pl.multiple_of(q * cr, cr), cr)
+        own = abuf[at, full:].astype(F32)
+        theirs = xsrc[ITERS % 2, at, 0:full].astype(F32)
+        sides = [own[:, :kh], theirs[:, :kh], own[:, kh:], theirs[:, kh:]]
+        turn_chunk(jnp.concatenate(sides, axis=1).astype(BF16), q)
         return 0
 
     lax.fori_loop(0, Q, wait_half, 0)
-    own = abuf[:, full:].astype(F32)
-    theirs = xsrc[ITERS % 2, :, 0:full].astype(F32)
-    turn(
-        jnp.concatenate(
-            [own[:, :kh], theirs[:, :kh], own[:, kh:], theirs[:, kh:]], axis=1
-        ).astype(BF16)
-    )
     f_copy.wait()
 
     def far(d, q):

time: 264 us -> 263 us (level)
  no operation moved by 1% of the time
where the time goes in v3:
time: 263 us
  Pallas kernels  260 us (99%)
  local copies, waits for them, and re-layouts  3.02 us (1%)
    pallas_call x1, Pallas kernels, on_device(): pl.pallas_call(functools.partial(kernel, n), out_shape=jax.ShapeDtypeStru...  260 us

profile of v3, /device:TPU:0, one launch (start us, length us, event | category | flops | bytes accessed | tf_op | source)
XLA Modules:
  0.0 262.5 jit_solution(2115915235676846234)
XLA Ops:
  0.0 1.3 copy.6.centres
  1.3 259.5 %shard_map.55 = f32[512,128]{1,0:T(8,128)} custom-call(bf16[1,2,4096,1024]{3,2,1,0:T(8,128)(2,1)} %tm.1, bf16[1,2,4096,1024]{3,2,1,0:T(8,128)(2,1)} %tr.1, bf16[2,2048,1024]{2,1,0:T(8,128)(2,1)} %ff.1, bf16[1,1024,256]{2,1,0:T(8,128)(2,1)} %e_hbm.1, s32[8,3]{1,0:T(8,128)} %copy.6.centres), custom_call_target="tpu_custom_call" | custom-call | tf_op jit(solution)/shard_map/pallas_call | solution.py:386
  260.9 1.7 copy.8
